TPU v7x, 256 devices: a whole 4x4x8 slice. The times are simulated.
256 devices in a mesh: fx: 8 (over z), fy: 16 (over x, y), grp: 2 (over core).
Axes of the slice: x: 4, y: 4, z: 8, core: 2. Of those that a mesh axis runs over, the one named last changes fastest.
Arguments:
- efield: float32 [3, 32, 128, 4096], P(None, None, 'fx', ('fy', 'grp')), may hold values from -6 to 6
- hfield: float32 [3, 32, 128, 4096], P(None, None, 'fx', ('fy', 'grp')), may hold values from -6 to 6
- loss_coef: float32 [32, 128, 4096], P(None, 'fx', ('fy', 'grp')), may hold values from 0.8 to 1
- update_coef: float32 [32, 128, 4096], P(None, 'fx', ('fy', 'grp')), may hold values from 0.2 to 0.6
- port_count: int32 [256], replicated, may hold values from 1 to 32, 4096 in all
- port_perm: int32 [4096], replicated, may hold values from 0 to 4095, each once
- port_cell: int32 [256, 32], P(('fx', 'fy', 'grp')), may hold values from 0 to 2047
- pole_state: float32 [2048, 256], P(('fx', 'fy', 'grp')), may hold values from -6 to 6
- transition: float32 [2048, 256, 256], P(('fx', 'fy', 'grp')), may hold values from -0.25 to 0.25
- input_map: float32 [2048, 256, 2], P(('fx', 'fy', 'grp')), may hold values from -6 to 6
- output_map: float32 [2048, 2, 256], P(('fx', 'fy', 'grp')), may hold values from -0.375 to 0.375
- feedthrough: float32 [2048, 2, 2], P(('fx', 'fy', 'grp')), may hold values from -4 to 4
Outputs:
- efield_out: float32 [3, 32, 128, 4096], P(None, None, 'fx', ('fy', 'grp'))
- hfield_out: float32 [3, 32, 128, 4096], P(None, None, 'fx', ('fy', 'grp'))
- final_state: float32 [2048, 256], P(('fx', 'fy', 'grp'))
Inputs may be any that keep to these rules, and one draw needn't show every extreme that they name: `port_count`: each tile holds between 1 and 32 ports, 4096 in all; some tile holds exactly 32. `port_perm`: each live port number once. `port_cell`: cell x * 128 + y within the tile; slots at or beyond the tile's port_count are unused.
All inputs are finite; a program needn't handle non-finite values.
Results may differ from a plain program's by a relative error of at most 0.0003.
Values sent between devices are 32-bit elements; how exact they have to be, the bound alone decides.
No kernel may reach another device: no remote copies, remote signals or barrier semaphores. Data moves between devices by JAX's collectives and lax.ppermute only.
A program may use at most 64 MiB of HBM per device.

v0:
```python
import jax
import jax.numpy as jnp
from jax import lax
from jax.sharding import PartitionSpec as P

K = 4
BLOCKS = 2


COURANT = 0.5
HIGH = lax.Precision.HIGHEST


def from_behind(value, axis, steps):
    count = lax.axis_size(axis)
    first, last = (max(0, -steps), min(count, count - steps))
    return lax.ppermute(value, axis, [(source, source + steps) for source in range(first, last)])


def forward(field, axis, after):
    ahead = jnp.concatenate(
        [lax.slice_in_dim(field, 1, field.shape[axis], axis=axis), after], axis=axis
    )
    return ahead - field


def backward(field, axis, before):
    behind = jnp.concatenate(
        [before, lax.slice_in_dim(field, 0, field.shape[axis] - 1, axis=axis)], axis=axis
    )
    return field - behind


def edge(field, axis):
    return jnp.zeros_like(lax.slice_in_dim(field, 0, 1, axis=axis))


def update_magnetic(electric, magnetic, next_x, next_y):
    elec_x, elec_y, elec_z = electric
    magn_x, magn_y, magn_z = magnetic
    flat = edge(elec_x, 0)
    magn_x = magn_x - COURANT * (forward(elec_z, 2, next_y[1]) - forward(elec_y, 0, flat))
    magn_y = magn_y - COURANT * (forward(elec_x, 0, flat) - forward(elec_z, 1, next_x[1]))
    magn_z = magn_z - COURANT * (forward(elec_y, 1, next_x[0]) - forward(elec_x, 2, next_y[0]))
    return (magn_x, magn_y, magn_z)


def update_electric(electric, magnetic, loss, gain, source, prev_x, prev_y):
    elec_x, elec_y, elec_z = electric
    magn_x, magn_y, magn_z = magnetic
    flat = edge(magn_x, 0)
    elec_x = loss * elec_x + gain * (backward(magn_z, 2, prev_y[1]) - backward(magn_y, 0, flat))
    elec_y = loss * elec_y + gain * (backward(magn_x, 0, flat) - backward(magn_z, 1, prev_x[1]))
    elec_z = loss * elec_z + gain * (
        backward(magn_y, 1, prev_x[0]) - backward(magn_x, 2, prev_y[0]) - source
    )
    return (elec_x, elec_y, elec_z)


def shifted_step(electric, magnetic, loss, gain, source):
    layers, rows, cols = electric[0].shape
    ahead_x = from_behind(jnp.stack([electric[1][:, 0, :], electric[2][:, 0, :]]), "fx", -1)
    ahead_y = from_behind(
        jnp.stack([electric[0][:, :, 0], electric[2][:, :, 0]]).reshape(-1), ("fy", "grp"), -1
    ).reshape(2, layers, rows)
    magnetic = update_magnetic(
        electric,
        magnetic,
        (ahead_x[0][:, None, :], ahead_x[1][:, None, :]),
        (ahead_y[0][:, :, None], ahead_y[1][:, :, None]),
    )
    behind_x = from_behind(jnp.stack([magnetic[1][:, -1, :], magnetic[2][:, -1, :]]), "fx", 1)
    behind_y = from_behind(
        jnp.stack([magnetic[0][:, :, -1], magnetic[2][:, :, -1]]).reshape(-1), ("fy", "grp"), 1
    ).reshape(2, layers, rows)
    electric = update_electric(
        electric,
        magnetic,
        loss,
        gain,
        source,
        (behind_x[0][:, None, :], behind_x[1][:, None, :]),
        (behind_y[0][:, :, None], behind_y[1][:, :, None]),
    )
    return (electric, magnetic)


def body(
    efield,
    hfield,
    loss_coef,
    update_coef,
    port_count,
    port_perm,
    port_cell,
    pole_state,
    transition,
    input_map,
    output_map,
    feedthrough,
):
    layers, rows, cols = (efield.shape[1], efield.shape[2], efield.shape[3])
    models = pole_state.shape[0]
    capacity = port_cell.shape[1]
    tile_total = lax.axis_size(("fx", "fy", "grp"))
    myself = lax.axis_index(("fx", "fy", "grp"))
    starts = jnp.cumsum(port_count) - port_count
    mine = lax.dynamic_slice_in_dim(port_perm, myself * (2 * models), 2 * models)
    tile_of = jnp.sum((starts[None, :] <= mine[:, None]).astype(jnp.int32), axis=1) - 1
    wanted = tile_of * capacity + (mine - starts[tile_of])
    cells = port_cell[0]
    placing = (cells[:, None] == jnp.arange(rows * cols, dtype=jnp.int32)[None, :]).astype(
        jnp.float32
    )
    electric = (efield[0], efield[1], efield[2])
    magnetic = (hfield[0], hfield[1], hfield[2])
    state = pole_state
    for block in range(BLOCKS):
        column = jnp.take(electric[2].reshape(layers, rows * cols), cells, axis=1)
        voltage_tile = jnp.mean(column, axis=0)
        everything = lax.all_gather(
            voltage_tile[None, :], ("fx", "fy", "grp"), axis=0, tiled=True
        ).reshape(-1)
        voltage = jnp.take(everything, wanted).reshape(models, 2)
        current = jnp.einsum("mqp,mp->mq", output_map, state, precision=HIGH) + jnp.einsum(
            "mqr,mr->mq", feedthrough, voltage, precision=HIGH
        )
        state = jnp.einsum("mpr,mr->mp", transition, state, precision=HIGH) + jnp.einsum(
            "mpq,mq->mp", input_map, voltage, precision=HIGH
        )
        target = wanted[:, None] == jnp.arange(tile_total * capacity, dtype=jnp.int32)[None, :]
        padded = jnp.sum(jnp.where(target, current.reshape(-1)[:, None], 0.0), axis=0)
        tile_current = lax.psum_scatter(
            padded.reshape(tile_total, capacity),
            ("fx", "fy", "grp"),
            scatter_dimension=0,
            tiled=True,
        )[0]
        source = jnp.dot(tile_current, placing, precision=HIGH).reshape(rows, cols)
        for step in range(K):
            electric, magnetic = shifted_step(electric, magnetic, loss_coef, update_coef, source)
    return (jnp.stack(electric), jnp.stack(magnetic), state)


def solution(mesh):
    return jax.shard_map(
        body,
        mesh=mesh,
        in_specs=(
            P(None, None, "fx", ("fy", "grp")),
            P(None, None, "fx", ("fy", "grp")),
            P(None, "fx", ("fy", "grp")),
            P(None, "fx", ("fy", "grp")),
            P(),
            P(),
            P(("fx", "fy", "grp"), None),
            P(("fx", "fy", "grp"), None),
            P(("fx", "fy", "grp"), None, None),
            P(("fx", "fy", "grp"), None, None),
            P(("fx", "fy", "grp"), None, None),
            P(("fx", "fy", "grp"), None, None),
        ),
        out_specs=(
            P(None, None, "fx", ("fy", "grp")),
            P(None, None, "fx", ("fy", "grp")),
            P(("fx", "fy", "grp"), None),
        ),
        check_vma=False,
    )
```

profile of v0, /device:TPU:89, one launch (start us, length us, event | category | flops | bytes accessed | tf_op | source)
XLA Modules:
  0.0 643.4 jit_solution(17622325822840929907)
XLA Ops:
  2.9 1.9 collective-permute-start
  5.4 2.7 collective-permute-start.1
  16.7 76.6 %all-reduce.32 = f32[8192]{0:T(1024)S(1)} all-reduce(f32[8192]{0:T(1024)S(1)} %multiply_dynamic-update-slice_fusion.1), channel_id=2, replica_groups=mesh['fx'=8,'fy'=16,'grp'=2] {'fx','fy','grp'}, use_global_device_ids=true, to_apply=%add.32 | all-reduce | flops 8192 | bytes 65536
  100.1 74.1 %all-reduce.34 = f32[256,32]{1,0:T(8,128)S(1)} all-reduce(f32[256,32]{1,0:T(8,128)S(1)} %reshape.515), channel_id=4, replica_groups=mesh['fx'=8,'fy'=16,'grp'=2] {'fx','fy','grp'}, use_global_device_ids=true, to_apply=%region_5.8.clone | all-reduce | flops 8192 | bytes 65536
  174.1 2.0 fusion.170
  176.2 2.1 copy_bitcast_fusion
  185.1 2.5 fusion.13
  188.3 3.6 collective-permute-start.2
  193.5 3.7 collective-permute-start.3
  199.7 2.1 fusion.16
  205.3 2.0 collective-permute-start.5
  214.9 3.9 collective-permute-start.4
  221.0 2.2 fusion.31
  224.7 6.0 collective-permute-start.6
  234.0 3.4 collective-permute-start.7
  239.7 2.0 fusion.34
  244.2 2.0 collective-permute-start.9
  258.4 2.2 fusion.49
  262.0 6.9 %collective-permute-start.10 = (f32[1024]{0:T(1024)S(1)}, f32[1024]{0:T(1024)S(1)}, u32[]{:S(2)}, u32[]{:S(2)}) collective-permute-start(f32[1024]{0:T(1024)S(1)} %reshape.519), channel_id=1, source_target_pairs={{0,1},{1,2},{2,3},{3,4},{4,5},{5,6},{6,7},{7,8},{8,9},{9,10},{10,1... | collective-permute-start | bytes 12296 | tf_op jit(solution)/shard_map/ppermute | solution.py:17
  272.3 3.7 collective-permute-start.11
  278.3 2.0 fusion.52
  295.9 2.3 fusion.67
  299.4 6.9 %collective-permute-start.14 = (f32[1024]{0:T(1024)S(1)}, f32[1024]{0:T(1024)S(1)}, u32[]{:S(2)}, u32[]{:S(2)}) collective-permute-start(f32[1024]{0:T(1024)S(1)} %reshape.521), channel_id=1, source_target_pairs={{0,1},{1,2},{2,3},{3,4},{4,5},{5,6},{6,7},{7,8},{8,9},{9,10},{10,1... | collective-permute-start | bytes 12296 | tf_op jit(solution)/shard_map/ppermute | solution.py:17
  308.6 3.6 collective-permute-start.15
  314.5 2.7 fusion.70
  319.6 1.9 gather_fusion.3
  321.9 72.8 %all-reduce.33 = f32[8192]{0:T(1024)S(1)} all-reduce(f32[8192]{0:T(1024)S(1)} %multiply_dynamic-update-slice_fusion), channel_id=3, replica_groups=mesh['fx'=8,'fy'=16,'grp'=2] {'fx','fy','grp'}, use_global_device_ids=true, to_apply=%add.33 | all-reduce | flops 8192 | bytes 65536
  402.1 2.6 collective-permute-start.17
  405.1 73.9 %all-reduce.35 = f32[256,32]{1,0:T(8,128)S(1)} all-reduce(f32[256,32]{1,0:T(8,128)S(1)} %reshape.527), channel_id=5, replica_groups=mesh['fx'=8,'fy'=16,'grp'=2] {'fx','fy','grp'}, use_global_device_ids=true, to_apply=%region_8.11.clone | all-reduce | flops 8192 | bytes 65536
  491.9 3.9 collective-permute-start.16
  498.8 2.2 fusion.85
  502.5 3.9 collective-permute-start.18
  509.8 3.7 collective-permute-start.19
  515.8 2.6 fusion.88
  521.8 2.0 collective-permute-start.21
  536.0 3.0 fusion.103
  540.1 6.9 %collective-permute-start.22 = (f32[1024]{0:T(1024)S(1)}, f32[1024]{0:T(1024)S(1)}, u32[]{:S(2)}, u32[]{:S(2)}) collective-permute-start(f32[1024]{0:T(1024)S(1)} %reshape.529), channel_id=1, source_target_pairs={{0,1},{1,2},{2,3},{3,4},{4,5},{5,6},{6,7},{7,8},{8,9},{9,10},{10,1... | collective-permute-start | bytes 12296 | tf_op jit(solution)/shard_map/ppermute | solution.py:17
  551.0 4.0 collective-permute-start.23
  557.3 2.8 fusion.112
  563.2 2.0 collective-permute-start.25
  578.8 2.2 fusion.126
  582.3 6.9 %collective-permute-start.26 = (f32[1024]{0:T(1024)S(1)}, f32[1024]{0:T(1024)S(1)}, u32[]{:S(2)}, u32[]{:S(2)}) collective-permute-start(f32[1024]{0:T(1024)S(1)} %reshape.531), channel_id=1, source_target_pairs={{0,1},{1,2},{2,3},{3,4},{4,5},{5,6},{6,7},{7,8},{8,9},{9,10},{10,1... | collective-permute-start | bytes 12296 | tf_op jit(solution)/shard_map/ppermute | solution.py:17
  592.5 3.6 collective-permute-start.27
  599.0 2.1 fusion.123
  603.7 2.1 collective-permute-start.29
  617.0 2.2 fusion.138
  622.9 6.9 %collective-permute-start.30 = (f32[1024]{0:T(1024)S(1)}, f32[1024]{0:T(1024)S(1)}, u32[]{:S(2)}, u32[]{:S(2)}) collective-permute-start(f32[1024]{0:T(1024)S(1)} %reshape.533), channel_id=1, source_target_pairs={{0,1},{1,2},{2,3},{3,4},{4,5},{5,6},{6,7},{7,8},{8,9},{9,10},{10,1... | collective-permute-start | bytes 12296 | tf_op jit(solution)/shard_map/ppermute | solution.py:17
  629.8 3.6 collective-permute-start.31
  (577 shorter events, 199.3 us)
Async XLA Ops:
  0.6 93.6 %copy-start = (f32[8,256,256]{2,1,0:T(8,128)S(1)}, f32[8,256,256]{2,1,0:T(8,128)}, u32[]{:S(2)}) copy-start(f32[8,256,256]{2,1,0:T(8,128)} %param.24) | copy-start | bytes 6291460
  2.0 183.1 %copy-start.54 = (f32[1,32,16,128]{3,2,1,0:T(8,128)}, f32[1,32,16,128]{3,2,1,0:T(8,128)S(1)}, u32[]{:S(2)}) copy-start(f32[1,32,16,128]{3,2,1,0:T(8,128)S(1)} %get-tuple-element.37) | copy-start | bytes 786436
  2.9 182.1 %collective-permute-start = (f32[2,32,128]{2,1,0:T(8,128)S(1)}, f32[2,32,128]{2,1,0:T(8,128)S(1)}, u32[]{:S(2)}, u32[]{:S(2)}) collective-permute-start(f32[2,32,128]{2,1,0:T(8,128)S(1)} %pad_maximum_fusion.2), channel_id=1, source_target_pairs={{32,0},{64,32},{96,64},{128,96},{160,128},{192,160},{224,192},{33,... | collective-permute-start | bytes 98312 | tf_op jit(solution)/shard_map/ppermute | solution.py:17
  5.1 88.9 %copy-start.66 = (f32[8,256]{1,0:T(8,128)S(1)}, f32[8,256]{1,0:T(8,128)}, u32[]{:S(2)}) copy-start(f32[8,256]{1,0:T(8,128)} %param.23) | copy-start | bytes 24580
  5.1 88.9 %copy-start.79 = (f32[8,2,256]{2,1,0:T(2,128)S(1)}, f32[8,2,256]{2,1,0:T(2,128)}, u32[]{:S(2)}) copy-start(f32[8,2,256]{2,1,0:T(2,128)} %param.26) | copy-start | bytes 49156
  5.4 176.6 %collective-permute-start.1 = (f32[1024]{0:T(1024)S(1)}, f32[1024]{0:T(1024)}, u32[]{:S(2)}, u32[]{:S(2)}) collective-permute-start(f32[1024]{0:T(1024)S(1)} %reshape.509), channel_id=1, source_target_pairs={{1,0},{2,1},{3,2},{4,3},{5,4},{6,5},{7,6},{8,7},{9,8},{10,9},{11,1... | collective-permute-start | bytes 12296 | tf_op jit(solution)/shard_map/ppermute | solution.py:17
  9.5 168.7 %copy-start.69 = (s32[16,128]{1,0:T(8,128)}, s32[16,128]{1,0:T(8,128)S(1)}, u32[]{:S(2)}) copy-start(s32[16,128]{1,0:T(8,128)S(1)} %multiply_add_fusion) | copy-start | bytes 24580
  9.6 86.6 %copy-start.80 = (f32[8,256,2]{1,2,0:T(2,128)S(1)}, f32[8,256,2]{1,2,0:T(2,128)}, u32[]{:S(2)}) copy-start(f32[8,256,2]{1,2,0:T(2,128)} %param.25) | copy-start | bytes 49156
  14.5 85.3 %copy-start.72 = (s32[16]{0:T(128)}, s32[16]{0:T(128)S(1)}, u32[]{:S(2)}) copy-start(s32[16]{0:T(128)S(1)} %get-tuple-element.9) | copy-start | bytes 196
  14.5 84.5 %copy-start.71 = (s32[1024]{0:T(1024)}, s32[1024]{0:T(1024)S(1)}, u32[]{:S(2)}) copy-start(s32[1024]{0:T(1024)S(1)} %pad_clamp_fusion) | copy-start | bytes 12292
  99.0 79.3 %copy-start.83 = (s32[1,32]{1,0:T(1,128)S(1)}, s32[1,32]{1,0:T(1,128)}, u32[]{:S(2)}) copy-start(s32[1,32]{1,0:T(1,128)} %param.22) | copy-start | bytes 388
  100.0 80.5 %copy-start.64 = (f32[32,16,128]{2,0,1:T(8,128)S(1)}, f32[32,16,128]{2,0,1:T(8,128)}, u32[]{:S(2)}) copy-start(f32[32,16,128]{2,0,1:T(8,128)} %copy-done.63) | copy-start | bytes 786436
  188.3 8.8 %collective-permute-start.2 = (f32[1024]{0:T(1024)S(1)}, f32[1024]{0:T(1024)S(1)}, u32[]{:S(2)}, u32[]{:S(2)}) collective-permute-start(f32[1024]{0:T(1024)S(1)} %reshape.510), channel_id=1, source_target_pairs={{0,1},{1,2},{2,3},{3,4},{4,5},{5,6},{6,7},{7,8},{8,9},{9,10},{10,1... | collective-permute-start | bytes 12296 | tf_op jit(solution)/shard_map/ppermute | solution.py:17
  193.5 6.2 collective-permute-start.3
  205.3 13.4 %collective-permute-start.5 = (f32[1024]{0:T(1024)S(1)}, f32[1024]{0:T(1024)S(1)}, u32[]{:S(2)}, u32[]{:S(2)}) collective-permute-start(f32[1024]{0:T(1024)S(1)} %reshape.516), channel_id=1, source_target_pairs={{1,0},{2,1},{3,2},{4,3},{5,4},{6,5},{7,6},{8,7},{9,8},{10,9},{11,1... | collective-permute-start | bytes 12296 | tf_op jit(solution)/shard_map/ppermute | solution.py:17
  214.9 6.1 collective-permute-start.4
  224.7 12.7 %collective-permute-start.6 = (f32[1024]{0:T(1024)S(1)}, f32[1024]{0:T(1024)S(1)}, u32[]{:S(2)}, u32[]{:S(2)}) collective-permute-start(f32[1024]{0:T(1024)S(1)} %reshape.517), channel_id=1, source_target_pairs={{0,1},{1,2},{2,3},{3,4},{4,5},{5,6},{6,7},{7,8},{8,9},{9,10},{10,1... | collective-permute-start | bytes 12296 | tf_op jit(solution)/shard_map/ppermute | solution.py:17
  234.0 5.6 collective-permute-start.7
  244.2 11.5 %collective-permute-start.9 = (f32[1024]{0:T(1024)S(1)}, f32[1024]{0:T(1024)S(1)}, u32[]{:S(2)}, u32[]{:S(2)}) collective-permute-start(f32[1024]{0:T(1024)S(1)} %reshape.518), channel_id=1, source_target_pairs={{1,0},{2,1},{3,2},{4,3},{5,4},{6,5},{7,6},{8,7},{9,8},{10,9},{11,1... | collective-permute-start | bytes 12296 | tf_op jit(solution)/shard_map/ppermute | solution.py:17
  253.7 4.6 collective-permute-start.8
  262.0 13.9 %collective-permute-start.10 = (f32[1024]{0:T(1024)S(1)}, f32[1024]{0:T(1024)S(1)}, u32[]{:S(2)}, u32[]{:S(2)}) collective-permute-start(f32[1024]{0:T(1024)S(1)} %reshape.519), channel_id=1, source_target_pairs={{0,1},{1,2},{2,3},{3,4},{4,5},{5,6},{6,7},{7,8},{8,9},{9,10},{10,1... | collective-permute-start | bytes 12296 | tf_op jit(solution)/shard_map/ppermute | solution.py:17
  272.3 5.9 collective-permute-start.11
  282.8 10.3 %collective-permute-start.13 = (f32[1024]{0:T(1024)S(1)}, f32[1024]{0:T(1024)S(1)}, u32[]{:S(2)}, u32[]{:S(2)}) collective-permute-start(f32[1024]{0:T(1024)S(1)} %reshape.520), channel_id=1, source_target_pairs={{1,0},{2,1},{3,2},{4,3},{5,4},{6,5},{7,6},{8,7},{9,8},{10,9},{11,1... | collective-permute-start | bytes 12296 | tf_op jit(solution)/shard_map/ppermute | solution.py:17
  291.2 4.6 collective-permute-start.12
  298.2 23.5 %copy-start.3 = (f32[32,16,128]{2,0,1:T(8,128)}, f32[32,16,128]{2,0,1:T(8,128)S(1)}, u32[]{:S(2)}) copy-start(f32[32,16,128]{2,0,1:T(8,128)S(1)} %get-tuple-element.55) | copy-start | bytes 786436
  299.4 12.9 %collective-permute-start.14 = (f32[1024]{0:T(1024)S(1)}, f32[1024]{0:T(1024)S(1)}, u32[]{:S(2)}, u32[]{:S(2)}) collective-permute-start(f32[1024]{0:T(1024)S(1)} %reshape.521), channel_id=1, source_target_pairs={{0,1},{1,2},{2,3},{3,4},{4,5},{5,6},{6,7},{7,8},{8,9},{9,10},{10,1... | collective-permute-start | bytes 12296 | tf_op jit(solution)/shard_map/ppermute | solution.py:17
  308.6 5.8 collective-permute-start.15
  317.2 78.2 %copy-start.73 = (s32[16]{0:T(128)S(1)}, s32[16]{0:T(128)}, u32[]{:S(2)}) copy-start(s32[16]{0:T(128)} %copy-done.72) | copy-start | bytes 196
  317.2 78.3 %copy-start.68 = (f32[8,2,2]{1,2,0:T(2,128)S(1)}, f32[8,2,2]{1,2,0:T(2,128)}, u32[]{:S(2)}) copy-start(f32[8,2,2]{1,2,0:T(2,128)} %copy-done.67) | copy-start | bytes 388
  317.2 78.5 %copy-start.81 = (f32[8,256,2]{1,2,0:T(2,128)S(1)}, f32[8,256,2]{1,2,0:T(2,128)}, u32[]{:S(2)}) copy-start(f32[8,256,2]{1,2,0:T(2,128)} %param.25) | copy-start | bytes 49156
  317.2 87.5 %copy-start.74 = (f32[8,1,2]{2,1,0:T(1,128)S(1)}, f32[8,1,2]{2,1,0:T(1,128)}, u32[]{:S(2)}) copy-start(f32[8,1,2]{2,1,0:T(1,128)} %fusion.158) | copy-start | bytes 196
  395.4 94.1 %copy-start.13 = (f32[32,16,128]{2,0,1:T(8,128)S(1)}, f32[32,16,128]{2,0,1:T(8,128)}, u32[]{:S(2)}) copy-start(f32[32,16,128]{2,0,1:T(8,128)} %get-tuple-element.20) | copy-start | bytes 786436
  402.1 93.7 %collective-permute-start.17 = (f32[1024]{0:T(1024)}, f32[1024]{0:T(1024)}, u32[]{:S(2)}, u32[]{:S(2)}) collective-permute-start(f32[1024]{0:T(1024)} %reshape.522), channel_id=1, source_target_pairs={{1,0},{2,1},{3,2},{4,3},{5,4},{6,5},{7,6},{8,7},{9,8},{10,9},{11,1... | collective-permute-start | bytes 12296 | tf_op jit(solution)/shard_map/ppermute | solution.py:17
  491.9 6.9 %collective-permute-start.16 = (f32[2,32,128]{2,1,0:T(8,128)S(1)}, f32[2,32,128]{2,1,0:T(8,128)S(1)}, u32[]{:S(2)}, u32[]{:S(2)}) collective-permute-start(f32[2,32,128]{2,1,0:T(8,128)S(1)} %pad_maximum_fusion.10), channel_id=1, source_target_pairs={{32,0},{64,32},{96,64},{128,96},{160,128},{192,160},{224,192},{33,... | collective-permute-start | bytes 98312 | tf_op jit(solution)/shard_map/ppermute | solution.py:17
  502.5 11.0 %collective-permute-start.18 = (f32[1024]{0:T(1024)S(1)}, f32[1024]{0:T(1024)S(1)}, u32[]{:S(2)}, u32[]{:S(2)}) collective-permute-start(f32[1024]{0:T(1024)S(1)} %reshape.523), channel_id=1, source_target_pairs={{0,1},{1,2},{2,3},{3,4},{4,5},{5,6},{6,7},{7,8},{8,9},{9,10},{10,1... | collective-permute-start | bytes 12296 | tf_op jit(solution)/shard_map/ppermute | solution.py:17
  509.8 6.0 collective-permute-start.19
  521.8 11.4 %collective-permute-start.21 = (f32[1024]{0:T(1024)S(1)}, f32[1024]{0:T(1024)S(1)}, u32[]{:S(2)}, u32[]{:S(2)}) collective-permute-start(f32[1024]{0:T(1024)S(1)} %reshape.528), channel_id=1, source_target_pairs={{1,0},{2,1},{3,2},{4,3},{5,4},{6,5},{7,6},{8,7},{9,8},{10,9},{11,1... | collective-permute-start | bytes 12296 | tf_op jit(solution)/shard_map/ppermute | solution.py:17
  531.3 4.6 collective-permute-start.20
  540.1 14.9 %collective-permute-start.22 = (f32[1024]{0:T(1024)S(1)}, f32[1024]{0:T(1024)S(1)}, u32[]{:S(2)}, u32[]{:S(2)}) collective-permute-start(f32[1024]{0:T(1024)S(1)} %reshape.529), channel_id=1, source_target_pairs={{0,1},{1,2},{2,3},{3,4},{4,5},{5,6},{6,7},{7,8},{8,9},{9,10},{10,1... | collective-permute-start | bytes 12296 | tf_op jit(solution)/shard_map/ppermute | solution.py:17
  551.0 6.2 collective-permute-start.23
  563.2 12.9 %collective-permute-start.25 = (f32[1024]{0:T(1024)S(1)}, f32[1024]{0:T(1024)S(1)}, u32[]{:S(2)}, u32[]{:S(2)}) collective-permute-start(f32[1024]{0:T(1024)S(1)} %reshape.530), channel_id=1, source_target_pairs={{1,0},{2,1},{3,2},{4,3},{5,4},{6,5},{7,6},{8,7},{9,8},{10,9},{11,1... | collective-permute-start | bytes 12296 | tf_op jit(solution)/shard_map/ppermute | solution.py:17
  574.1 4.6 collective-permute-start.24
  582.3 14.7 %collective-permute-start.26 = (f32[1024]{0:T(1024)S(1)}, f32[1024]{0:T(1024)S(1)}, u32[]{:S(2)}, u32[]{:S(2)}) collective-permute-start(f32[1024]{0:T(1024)S(1)} %reshape.531), channel_id=1, source_target_pairs={{0,1},{1,2},{2,3},{3,4},{4,5},{5,6},{6,7},{7,8},{8,9},{9,10},{10,1... | collective-permute-start | bytes 12296 | tf_op jit(solution)/shard_map/ppermute | solution.py:17
  592.5 6.4 collective-permute-start.27
  603.7 10.6 %collective-permute-start.29 = (f32[1024]{0:T(1024)S(1)}, f32[1024]{0:T(1024)S(1)}, u32[]{:S(2)}, u32[]{:S(2)}) collective-permute-start(f32[1024]{0:T(1024)S(1)} %reshape.532), channel_id=1, source_target_pairs={{1,0},{2,1},{3,2},{4,3},{5,4},{6,5},{7,6},{8,7},{9,8},{10,9},{11,1... | collective-permute-start | bytes 12296 | tf_op jit(solution)/shard_map/ppermute | solution.py:17
  612.3 4.6 collective-permute-start.28
  622.9 14.8 %collective-permute-start.30 = (f32[1024]{0:T(1024)S(1)}, f32[1024]{0:T(1024)S(1)}, u32[]{:S(2)}, u32[]{:S(2)}) collective-permute-start(f32[1024]{0:T(1024)S(1)} %reshape.533), channel_id=1, source_target_pairs={{0,1},{1,2},{2,3},{3,4},{4,5},{5,6},{6,7},{7,8},{8,9},{9,10},{10,1... | collective-permute-start | bytes 12296 | tf_op jit(solution)/shard_map/ppermute | solution.py:17
  629.8 9.9 %collective-permute-start.31 = (f32[2,32,128]{2,1,0:T(8,128)S(1)}, f32[2,32,128]{2,1,0:T(8,128)S(1)}, u32[]{:S(2)}, u32[]{:S(2)}) collective-permute-start(f32[2,32,128]{2,1,0:T(8,128)S(1)} %pad_maximum_fusion.17), channel_id=1, source_target_pairs={{0,32},{32,64},{64,96},{96,128},{128,160},{160,192},{192,224},{1,3... | collective-permute-start | bytes 98312 | tf_op jit(solution)/shard_map/ppermute | solution.py:17
  (68 other events, 354.3 us)
where the time goes:
time: 655 us; the launch traced here: 643 us
  blocking collectives  297 us (45%)
  local copies, waits for them, and re-layouts  170 us (26%)
  starting transfers between devices  114 us (17%)
  other arithmetic  48 us (7%)
  matrix products  8.21 us (1%)
    unnamed x4, blocking collectives  297 us
    ppermute x32, starting transfers between devices, from_behind(): lax.ppermute(value, axis, [(source, source + steps) for source in range(f...  114 us
    slice x48, local copies, waits for them, and re-layouts, forward(): lax.slice_in_dim(field, 1, field.shape[axis], axis=axis)  59.2 us
    slice x18, local copies, waits for them, and re-layouts, backward(): lax.slice_in_dim(field, 0, field.shape[axis] - 1, axis=axis)  21.3 us
    sub x8, other arithmetic, update_magnetic(): magn_x - COURANT * (forward(elec_z, 2, next_y[1]) - forward(elec_y, 0, fl...  15 us
    add x6, other arithmetic, update_electric(): loss * elec_x  13.6 us
  transfers between devices with their start and end apart: 32, of which 6 were waited for; matrix products, arithmetic and copies ran while one was open for 22% of the time, Pallas kernels for 0%

commit v1 on v0

v1 whole, which is shorter than its diff:
```python
import functools

import jax
import jax.numpy as jnp
from jax import lax
from jax.experimental import pallas as pl
from jax.experimental.pallas import tpu as pltpu
from jax.sharding import PartitionSpec as P

K = 4
BLOCKS = 2
COURANT = 0.5
HIGH = lax.Precision.HIGHEST
ALL = ("fx", "fy", "grp")
Z, X, Y = 32, 16, 128
SLOTS = 32
LIST = 9 * SLOTS
MODELS = 8
F32 = jnp.float32
I32 = jnp.int32
LANE_O, LANE_D, LANE_C = 32, 48, 80
OWN, MATE, DRAWN, SELF, CROSS, CELL, MASKS = 0, 288, 592, 880, 1168, 1456, 1744
STRIP = 16 * Z
LAG_E, LAG_H = 6, 4


def iota(shape, dim):
    return lax.broadcasted_iota(I32, shape, dim)


class Copies:
    def __init__(self, sems):
        self.sems, self.used, self.open = sems, 0, []

    def start(self, source, target):
        copy = pltpu.make_async_copy(source, target, self.sems.at[self.used])
        self.used += 1
        copy.start()
        self.open.append(copy)

    def group(self):
        group, self.open = self.open, []
        return group

    def wait(self, group=None):
        for copy in self.group() if group is None else group:
            copy.wait()


def port_means(mean, cells):
    pick_y = (iota((Y, SLOTS), 0) == cells % Y).astype(F32)
    columns = jnp.dot(mean, pick_y, precision=HIGH, preferred_element_type=F32)
    return jnp.sum(jnp.where(iota((X, SLOTS), 0) == cells // Y, columns, 0.0), axis=0, keepdims=True)


def drawn_lanes(output_ref, state):
    lane, model = iota((MODELS, Y), 1), iota((MODELS, Y), 0)
    row = jnp.zeros((1, Y), F32)
    for q in range(2):
        drawn = jnp.sum(output_ref[:, q, :] * state, axis=1, keepdims=True)
        row = row + jnp.sum(
            jnp.where(lane == LANE_O + 2 * model + q, drawn, 0.0), axis=0, keepdims=True
        )
    return row


def pack_rows(read, up_ref, down_ref, c):
    low = iota((8, Y), 0) < 4
    for z in range(Z // 2):
        a, b = read(z), read(z + Z // 2)
        up_ref[16 * c + z] = jnp.where(low, a[:8], pltpu.roll(b[:8], 4, 0))
        down_ref[16 * c + z] = jnp.where(low, pltpu.roll(b[8:], 4, 0), a[8:])


def load_parts(copies, e_hbm, h_hbm, loss_hbm, gain_hbm, parts):
    sources = [e_hbm.at[c] for c in range(3)] + [h_hbm.at[c] for c in range(3)] + [loss_hbm, gain_hbm]
    groups = []
    for c, source in enumerate(sources):
        copies.start(source, parts.at[c])
        groups.append(copies.group())
    return groups


def pack_kernel(e_hbm, h_hbm, loss_hbm, gain_hbm, up_out, down_out, parts, up, down, sems):
    copies = Copies(sems)
    groups = load_parts(copies, e_hbm, h_hbm, loss_hbm, gain_hbm, parts)
    for c in range(8):
        copies.wait(groups[c])
        pack_rows(lambda z: parts[c, z], up, down, c)
        own = pl.ds(16 * c, 16)
        copies.start(up.at[own], up_out.at[own])
        copies.start(down.at[own], down_out.at[own])
    copies.wait()


def row_kernel(
    feed_hbm, e_hbm, cells_hbm, state_hbm, output_hbm, after_hbm, row_out, fixed_out,
    feed, ez, cells, state, output, line, row, fixed, sems,
):
    copies = Copies(sems)
    pairs = ((feed_hbm, feed), (e_hbm.at[2], ez), (cells_hbm, cells), (state_hbm, state), (output_hbm, output))
    for source, target in pairs:
        copies.start(source, target)
    copies.wait()
    mean = ez[0]
    for z in range(1, Z):
        mean = mean + ez[z]
    line[...] = jnp.zeros_like(line)
    line[0:1, :SLOTS] = cells[...].astype(F32)
    for k in range(4):
        line[k + 1 : k + 2, :MODELS] = feed[k // 2, k % 2 : k % 2 + 1, :]
    lines = line[...]
    total = pltpu.roll(lines, LANE_C, 1)[0:1]
    for k in range(4):
        total = total + pltpu.roll(lines, LANE_D + 8 * k, 1)[k + 1 : k + 2]
    fixed[...] = total
    row[...] = jnp.broadcast_to(total + drawn_lanes(output, state[...]), row.shape)
    row[:, :SLOTS] = jnp.broadcast_to(port_means(mean * (1.0 / Z), cells[...]), (256, SLOTS))
    copies.start(row, row_out)
    copies.start(fixed, fixed_out)
    copies.wait()


def side_kernel(
    e_hbm, h_hbm, loss_hbm, gain_hbm, after_hbm, before_hbm, row_hbm, halo_out, pack_out,
    parts, after, before, halo, pack, sems,
):
    copies = Copies(sems)
    copies.start(after_hbm, after)
    copies.start(before_hbm, before)
    received = copies.group()
    groups = load_parts(copies, e_hbm, h_hbm, loss_hbm, gain_hbm, parts)
    copies.wait(received)
    low = iota((8, Y), 0) < 4
    group = iota((8, Y), 1) // 16
    for c in range(8):
        copies.wait(groups[c])
        for z in range(Z // 2):
            a, b = after[16 * c + z], before[16 * c + z]
            halo[c, z] = jnp.where(low, a, b)
            halo[c, z + Z // 2] = pltpu.roll(jnp.where(low, b, a), 4, 0)
        for part in range(4):
            total = [jnp.zeros((8, Y), F32)] * 3
            for zl in range(8):
                z = part * 8 + zl
                plane = parts[c, z]
                for i, tile in enumerate((plane[:8], plane[8:], halo[c, z])):
                    moved = pltpu.roll(tile, (16 * zl + 8) % Y, 1)
                    total[i] = jnp.where(group == zl, moved, total[i])
            for i in range(3):
                pack[c, 8 * i : 8 * i + 8, Y * part : Y * part + Y] = total[i]
        copies.start(pack.at[c], pack_out.at[c])
        copies.start(halo.at[c], halo_out.at[c])
    copies.wait()


def index_kernel(counts_hbm, perm_hbm, pick_out, mask_out, counts_ref, perm_ref, pick, mask, sems):
    copies = Copies(sems)
    copies.start(counts_hbm, counts_ref)
    copies.start(perm_hbm, perm_ref)
    copies.wait()
    me, fx, fy = lax.axis_index(ALL), lax.axis_index("fx"), lax.axis_index(("fy", "grp"))
    counts = counts_ref[...]
    starts = counts
    for width in (1, 2, 4, 8, 16, 32, 64, 128):
        starts = starts + jnp.where(iota((1, 256), 1) >= width, pltpu.roll(starts, width, 1), 0)
    starts = starts - counts
    number = iota((LIST, 1), 0)
    slot = number % SLOTS
    dx, dy = number // SLOTS // 3 - 1, number // SLOTS % 3 - 1
    inside = (fx + dx >= 0) & (fx + dx < 8) & (fy + dy >= 0) & (fy + dy < 32)
    tile = jnp.where(inside, me + 32 * dx + dy, -1)
    own = iota((LIST, 256), 1) == tile
    start = jnp.sum(jnp.where(own, starts, 0), axis=1, keepdims=True)
    count = jnp.sum(jnp.where(own, counts, 0), axis=1, keepdims=True)
    live = slot < count
    wanted = jnp.where(live, start + slot, -1)
    even = iota((32, Y), 1) % 2 == 0
    perm = perm_ref[...]
    mates = jnp.where(even, pltpu.roll(perm, Y - 1, 1), pltpu.roll(perm, 1, 1))
    position = jnp.zeros((LIST, Y), I32)
    partner = jnp.zeros((LIST, Y), I32)
    spot = iota((2 * MODELS, Y), 0)
    mine_at = me * 2 * MODELS + 2 * (spot % MODELS) + spot // MODELS
    mine = jnp.zeros((2 * MODELS, Y), I32)
    for r in range(32):
        row, mate = perm[r : r + 1], mates[r : r + 1]
        hit = row == wanted
        position = jnp.where(hit, iota((LIST, Y), 1) + Y * r, position)
        partner = jnp.where(hit, mate, partner)
        mine = jnp.where(iota((2 * MODELS, Y), 1) + Y * r == mine_at, row, mine)
    position = jnp.sum(position, axis=1, keepdims=True)
    partner = jnp.sum(partner, axis=1, keepdims=True)
    mine = jnp.sum(mine, axis=1, keepdims=True)
    ports = jnp.concatenate([partner, mine], axis=0)
    total = LIST + 2 * MODELS
    before = starts <= ports
    port_tile = jnp.sum(before.astype(I32), axis=1, keepdims=True) - 1
    port_start = jnp.max(jnp.where(before, starts, 0), axis=1, keepdims=True)
    port_slot = ports - port_start
    pick[:LIST] = own.astype(F32).astype(jnp.bfloat16)
    pick[LIST : LIST + total] = (iota((total, 256), 1) == port_tile).astype(F32).astype(jnp.bfloat16)
    pick[LIST + total :] = (iota((LIST, 256), 1) == position // 16).astype(F32).astype(jnp.bfloat16)
    lane = iota((LIST, Y), 1)
    q = position % 2
    model = position // 2 % MODELS
    on = live.astype(F32)
    mask[OWN:MATE] = jnp.where(lane == slot, on, 0.0)
    mask[MATE:DRAWN] = (iota((total, Y), 1) == port_slot).astype(F32)
    mask[DRAWN:SELF] = jnp.where(lane == LANE_O + 2 * model + q, on, 0.0)
    mask[SELF:CROSS] = jnp.where(lane == LANE_D + 24 * q + model, on, 0.0)
    mask[CROSS:CELL] = jnp.where(lane == LANE_D + 8 * (q + 1) + model, on, 0.0)
    mask[CELL:] = (lane == LANE_C + slot).astype(F32)
    copies.start(pick, pick_out)
    copies.start(mask, mask_out)
    copies.wait()


def port_sources(gathered_ref, pick_ref, mask_ref):
    gathered = gathered_ref[...]
    high = gathered.astype(jnp.bfloat16)
    left_over = gathered - high.astype(F32)
    middle = left_over.astype(jnp.bfloat16)
    low = (left_over - middle.astype(F32)).astype(jnp.bfloat16)
    picked = jnp.dot(
        pick_ref[...], jnp.concatenate([high, middle, low], axis=1), preferred_element_type=F32
    )
    picked = picked[:, :Y] + picked[:, Y : 2 * Y] + picked[:, 2 * Y :]
    total = LIST + 2 * MODELS

    def choose(part, mask):
        return jnp.sum(part * mask, axis=1, keepdims=True)

    of_tile, of_port, of_model = picked[:LIST], picked[LIST : LIST + total], picked[LIST + total :]
    own = choose(of_tile, mask_ref[OWN:MATE])
    others = choose(of_port, mask_ref[MATE:DRAWN])
    mate, mine = others[:LIST], others[LIST:]
    current = choose(
        of_model, mask_ref[DRAWN:SELF] + mask_ref[SELF:CROSS] * own + mask_ref[CROSS:CELL] * mate
    )
    cell = choose(of_tile, mask_ref[CELL:]).astype(I32)
    number = iota((LIST, 1), 0) // SLOTS
    x = (number // 3 - 1) * X + cell // Y
    y = (number % 3 - 1) * Y + cell % Y
    lane = iota((LIST, 2 * Y), 1)
    lane_y = jnp.where(lane < Y, lane, jnp.where(lane < Y + 16, lane - 136, jnp.where(lane < Y + 32, lane - 24, -1000)))
    row = iota((LIST, Y), 1)
    row_x = jnp.where(row < 20, row, jnp.where(row < 24, row - 24, -1000))
    spread = jnp.where(lane_y == y, current, 0.0)
    to_row = (row_x == x).astype(F32)
    source = lax.dot_general(
        to_row, spread, (((0,), (0,)), ((), ())), precision=HIGH, preferred_element_type=F32
    )[:24]
    return source, mine


def repeat_groups(row_lanes):
    value = jnp.where(iota(row_lanes.shape, 1) < 16, row_lanes, 0.0)
    for width in (16, 32, 64):
        value = value + pltpu.roll(value, width, 1)
    return jnp.concatenate([value] * 4, axis=1)


def strip_step(fields, loss, gain, drive, keep_x, z_first, z_last):
    ex, ey, ez, hx, hy, hz = fields

    def up(v):
        return jnp.where(z_last, 0.0, pltpu.roll(v, STRIP - 16, 1))

    def down(v):
        return jnp.where(z_first, 0.0, pltpu.roll(v, 16, 1))

    hx = hx - COURANT * ((pltpu.roll(ez, STRIP - 1, 1) - ez) - (up(ey) - ey))
    hy = (hy - COURANT * ((up(ex) - ex) - (pltpu.roll(ez, 23, 0) - ez))) * keep_x
    hz = (hz - COURANT * ((pltpu.roll(ey, 23, 0) - ey) - (pltpu.roll(ex, STRIP - 1, 1) - ex))) * keep_x
    ex = loss * ex + gain * ((hz - pltpu.roll(hz, 1, 1)) - (hy - down(hy)))
    ey = loss * ey + gain * ((hx - down(hx)) - (hz - pltpu.roll(hz, 1, 0)))
    ez = loss * ez + gain * ((hy - pltpu.roll(hy, 1, 0)) - (hx - pltpu.roll(hx, 1, 1)) - drive)
    return [ex, ey, ez, hx, hy, hz]


def block_kernel(last, *refs):
    refs = list(refs)

    def take(n):
        got = refs[:n]
        del refs[:n]
        return got

    e_hbm, h_hbm, loss_hbm, gain_hbm, halo_hbm = take(5)
    packs_hbm = take(3)
    shared_hbm = take(8)
    if last:
        strips_hbm, after_hbm, before_hbm = take(3)
    e_out, h_out, state_out = take(3)
    if not last:
        row_out, up_out, down_out, strips_out = take(4)
    state, coef, seam, strips = take(4)
    packs = take(3)
    gathered, pick, mask, cells, fixed, moved, inputs, output = take(8)
    row, up, down, new_state, sems = take(5)
    fx, fy = lax.axis_index("fx"), lax.axis_index(("fy", "grp"))

    copies = Copies(sems)
    for source, target in zip(shared_hbm, (gathered, pick, mask, cells, fixed, moved, inputs, output)):
        copies.start(source, target)
    shared = copies.group()
    if last:
        for source, target in zip(packs_hbm, packs):
            copies.start(source.at[pl.ds(6, 2)], target.at[pl.ds(6, 2)])
        copies.start(strips_hbm, strips.at[:, pl.ds(0, X)])
        copies.start(after_hbm, up)
        copies.start(before_hbm, down)
    else:
        for source, target in zip(packs_hbm, packs):
            copies.start(source, target)
    edges = copies.group()
    for c in range(3):
        copies.start(e_hbm.at[c], state.at[c, pl.ds(0, Z), pl.ds(0, X)])
        copies.start(h_hbm.at[c], state.at[3 + c, pl.ds(1, Z), pl.ds(0, X)])
    copies.start(loss_hbm, coef.at[0, :, pl.ds(0, X)])
    copies.start(gain_hbm, coef.at[1, :, pl.ds(0, X)])
    for i in range(2):
        copies.start(halo_hbm.at[6 + i], coef.at[i, :, pl.ds(X, 8)])
    if not last:
        for c in range(6):
            copies.start(halo_hbm.at[c], state.at[c, pl.ds(c // 3, Z), pl.ds(X, 8)])
    fields = copies.group()
    for c in range(3):
        state[c, Z] = jnp.zeros((24, Y), F32)
        state[3 + c, 0] = jnp.zeros((24, Y), F32)
    copies.wait(shared)
    source, mine = port_sources(gathered, pick, mask)
    new_state[...] = (
        moved[...] + inputs[:, 0, :] * mine[:MODELS] + inputs[:, 1, :] * mine[MODELS:]
    )
    copies.start(new_state, state_out)
    copies.wait(edges)

    own, left, right = packs
    lanes = iota((24, STRIP), 1)
    before_half = lanes % 16 < 8
    low_coefs = [jnp.where(before_half, left[c], own[c]) for c in (6, 7)]
    high_coefs = [jnp.where(before_half, own[c], right[c]) for c in (6, 7)]
    if last:
        low = iota((8, Y), 0) < 4
        for c in range(6):
            for z in range(Z // 2):
                a, b = up[16 * c + z], down[16 * c + z]
                state[c, z + c // 3, X:] = jnp.where(low, a, b)
                state[c, z + Z // 2 + c // 3, X:] = pltpu.roll(jnp.where(low, b, a), 4, 0)
        for i in range(12):
            for j in range(2):
                a, b = up[96 + 2 * i + j], down[96 + 2 * i + j]
                strips[i, X:, Y * j : Y * j + Y] = jnp.where(low, a, b)
                strips[i, X:, Y * (j + 2) : Y * (j + 3)] = pltpu.roll(jnp.where(low, b, a), 4, 0)
    else:
        for c in range(6):
            strips[c] = jnp.where(before_half, left[c], own[c])
            strips[6 + c] = jnp.where(before_half, own[c], right[c])

    keep_x = jnp.where((iota((24, 1), 0) >= 20) & (fx == 0), 0.0, 1.0)
    keep_y = jnp.where(fy == 0, 0.0, 1.0)
    z_last, z_first = lanes >= STRIP - 16, lanes < 16
    at_seam = lanes % 16 == 8
    low_drive = repeat_groups(source[:, Y:])
    high_drive = repeat_groups(pltpu.roll(source[:, Y:], Y - 16, 1))

    def strips_step(s, carry):
        low_next = strip_step(
            [strips[c] for c in range(6)], *low_coefs, low_drive, keep_x, z_first, z_last
        )
        for i, (e_at, h_at) in enumerate(((2, 3), (0, 5))):
            joined = jnp.where(at_seam, strips[6 + e_at], pltpu.roll(low_next[h_at] * keep_y, 2, 1))
            for part in range(4):
                seam[s, i, part] = joined[:, Y * part : Y * part + Y]
        high_next = strip_step(
            [strips[6 + c] for c in range(6)], *high_coefs, high_drive, keep_x, z_first, z_last
        )
        for c in range(6):
            strips[c] = low_next[c]
            strips[6 + c] = high_next[c]
        return carry

    lax.fori_loop(0, K, strips_step, 0)

    if not last:
        copies.start(strips.at[:, pl.ds(0, X)], strips_out)
        low = iota((8, Y), 0) < 4
        for i in range(12):
            for j in range(2):
                a, b = (strips[i, :X, Y * k : Y * k + Y] for k in (j, j + 2))
                up[96 + 2 * i + j] = jnp.where(low, a[:8], pltpu.roll(b[:8], 4, 0))
                down[96 + 2 * i + j] = jnp.where(low, pltpu.roll(b[8:], 4, 0), a[8:])
    copies.wait(fields)

    main_source = source[:, :Y]
    lane = iota((24, Y), 1)
    end, begin = lane == Y - 1, lane == 0

    def step(s, carry):
        def turned(z):
            turn = (247 - 16 * (z % 8)) % Y
            return pltpu.roll(seam[s, 0, z // 8], turn, 1), pltpu.roll(seam[s, 1, z // 8], turn, 1)

        def shift_electric(z):
            seam_a, seam_b = turned(z)
            return (
                jnp.where(end, seam_a, pltpu.roll(state[2, z], Y - 1, 1)),
                jnp.where(end, seam_b, pltpu.roll(state[0, z], Y - 1, 1)),
                seam_a,
                seam_b,
            )

        def magnetic(z, ez_next, ex_next, seam_a, seam_b):
            ex, ey, ez = state[0, z], state[1, z], state[2, z]
            hx = state[3, z + 1] - COURANT * ((ez_next - ez) - (state[1, z + 1] - ey))
            hy = state[4, z + 1] - COURANT * ((state[0, z + 1] - ex) - (pltpu.roll(ez, 23, 0) - ez))
            hz = state[5, z + 1] - COURANT * ((pltpu.roll(ey, 23, 0) - ey) - (ex_next - ex))
            hy = hy * keep_x
            hz = hz * keep_x
            state[3, z + 1] = hx
            state[4, z + 1] = hy
            state[5, z + 1] = hz
            return (
                jnp.where(begin, seam_a, pltpu.roll(hx, 1, 1)),
                jnp.where(begin, seam_b, pltpu.roll(hz, 1, 1)),
            )

        def electric(z, hx_before, hz_before):
            hx, hy, hz = state[3, z + 1], state[4, z + 1], state[5, z + 1]
            loss, gain = coef[0, z], coef[1, z]
            state[0, z] = loss * state[0, z] + gain * ((hz - hz_before) - (hy - state[4, z]))
            state[1, z] = loss * state[1, z] + gain * (
                (hx - state[3, z]) - (hz - pltpu.roll(hz, 1, 0))
            )
            state[2, z] = loss * state[2, z] + gain * (
                (hy - pltpu.roll(hy, 1, 0)) - (hx - hx_before) - main_source
            )

        shifted, magnetics = {}, {}
        for t in range(Z + LAG_E + LAG_H):
            if t < Z:
                shifted[t] = shift_electric(t)
            if 0 <= t - LAG_E < Z:
                magnetics[t - LAG_E] = magnetic(t - LAG_E, *shifted.pop(t - LAG_E))
            if 0 <= t - LAG_E - LAG_H:
                electric(t - LAG_E - LAG_H, *magnetics.pop(t - LAG_E - LAG_H))
        return carry

    lax.fori_loop(0, K, step, 0)

    for c in range(3):
        copies.start(state.at[c, pl.ds(0, Z), pl.ds(0, X)], e_out.at[c])
        copies.start(state.at[3 + c, pl.ds(1, Z), pl.ds(0, X)], h_out.at[c])
    if not last:
        for c in range(6):
            pack_rows(lambda z: state[c, z + c // 3, :X], up, down, c)
        copies.start(up, up_out)
        copies.start(down, down_out)
        mean = state[2, 0, :X]
        for z in range(1, Z):
            mean = mean + state[2, z, :X]
        row[...] = jnp.broadcast_to(fixed[...] + drawn_lanes(output, new_state[...]), row.shape)
        row[:, :SLOTS] = jnp.broadcast_to(port_means(mean * (1.0 / Z), cells[...]), (256, SLOTS))
        copies.start(row, row_out)
    copies.wait()


def shape(*dims, dtype=F32):
    return jax.ShapeDtypeStruct(dims, dtype)


def call(kernel, outs, scratch, cost=1_000_000):
    scratch = [pltpu.VMEM(dims, F32) if isinstance(dims, tuple) else dims for dims in scratch]
    place = pl.BlockSpec(memory_space=pl.ANY)

    def run(*args):
        return pl.pallas_call(
            kernel,
            out_shape=outs,
            in_specs=[place] * len(args),
            out_specs=jax.tree.map(lambda _: place, outs),
            scratch_shapes=scratch + [pltpu.SemaphoreType.DMA((64,))],
            compiler_params=pltpu.CompilerParams(vmem_limit_bytes=56 * 1024 * 1024),
            cost_estimate=pl.CostEstimate(flops=cost, bytes_accessed=cost, transcendentals=0),
        )(*args)

    return run


def neighbours(up, down):
    after = lax.ppermute(up, "fx", [(i + 1, i) for i in range(7)])
    before = lax.ppermute(down, "fx", [(i, i + 1) for i in range(7)])
    return after, before


def sides(pack):
    axes = ("fy", "grp")
    left = lax.ppermute(pack, axes, [(i, i + 1) for i in range(31)])
    right = lax.ppermute(pack, axes, [(i + 1, i) for i in range(31)])
    return left, right


def exchange(row):
    return lax.all_to_all(row, ALL, 0, 0, tiled=True)


def body(
    efield, hfield, loss, gain, port_count, port_perm, port_cell,
    pole_state, transition, input_map, output_map, feedthrough,
):
    inputs = jnp.swapaxes(input_map, 1, 2)
    feed = jnp.transpose(feedthrough, (1, 2, 0))
    ints = functools.partial(pltpu.VMEM, dtype=I32)
    picks = 2 * LIST + LIST + 2 * MODELS
    tiles8, tiles6 = (128, 8, Y), (120, 8, Y)

    up, down = call(
        pack_kernel, (shape(*tiles8), shape(*tiles8)), [(8, Z, X, Y), tiles8, tiles8]
    )(efield, hfield, loss, gain)
    after, before = neighbours(up, down)
    row, fixed = call(
        row_kernel,
        (shape(256, Y), shape(1, Y)),
        [(2, 2, MODELS), (Z, X, Y), ints((1, SLOTS)), (MODELS, 256), (MODELS, 2, 256), (8, Y), (256, Y), (1, Y)],
    )(feed, efield, port_cell, pole_state, output_map, up)
    gathered = exchange(row)
    pick, mask = call(
        index_kernel,
        (shape(picks, 256, dtype=jnp.bfloat16), shape(MASKS, Y)),
        [ints((1, 256)), ints((32, Y)), pltpu.VMEM((picks, 256), jnp.bfloat16), (MASKS, Y)],
    )(port_count.reshape(1, 256), port_perm.reshape(32, Y))
    halo, pack = call(
        side_kernel,
        (shape(8, Z, 8, Y), shape(8, 24, STRIP)),
        [(8, Z, X, Y), tiles8, tiles8, (8, Z, 8, Y), (8, 24, STRIP)],
    )(efield, hfield, loss, gain, after, before, row)
    left, right = sides(pack)
    moved = jnp.einsum("mpr,mr->mp", transition, pole_state, precision=HIGH)

    scratch = (
        [(6, Z + 1, 24, Y), (2, Z, 24, Y), (K, 2, 4, 24, Y), (12, 24, STRIP)]
        + [(8, 24, STRIP)] * 3
        + [(256, Y), pltpu.VMEM((picks, 256), jnp.bfloat16), (MASKS, Y), ints((1, SLOTS)), (1, Y)]
        + [(MODELS, 256), (MODELS, 2, 256), (MODELS, 2, 256), (256, Y), tiles6, tiles6, (MODELS, 256)]
    )
    field = (shape(3, Z, X, Y), shape(3, Z, X, Y), shape(MODELS, 256))
    electric, magnetic, state, row, up, down, strips = call(
        functools.partial(block_kernel, False),
        field + (shape(256, Y), shape(*tiles6), shape(*tiles6), shape(12, X, STRIP)),
        scratch,
    )(
        efield, hfield, loss, gain, halo, pack, left, right,
        gathered, pick, mask, port_cell, fixed, moved, inputs, output_map,
    )

    after, before = neighbours(up, down)
    gathered = exchange(row)
    moved = jnp.einsum("mpr,mr->mp", transition, state, precision=HIGH)
    return call(functools.partial(block_kernel, True), field, scratch)(
        electric, magnetic, loss, gain, halo, pack, left, right,
        gathered, pick, mask, port_cell, fixed, moved, inputs, output_map, strips, after, before,
    )


def solution(mesh):
    return jax.shard_map(
        body,
        mesh=mesh,
        in_specs=(
            P(None, None, "fx", ("fy", "grp")),
            P(None, None, "fx", ("fy", "grp")),
            P(None, "fx", ("fy", "grp")),
            P(None, "fx", ("fy", "grp")),
            P(),
            P(),
            P(ALL, None),
            P(ALL, None),
            P(ALL, None, None),
            P(ALL, None, None),
            P(ALL, None, None),
            P(ALL, None, None),
        ),
        out_specs=(
            P(None, None, "fx", ("fy", "grp")),
            P(None, None, "fx", ("fy", "grp")),
            P(ALL, None),
        ),
        check_vma=False,
    )
```

time: 655 us -> 111 us (0.17)
  the two profiles are of different devices: /device:TPU:89 before, /device:TPU:1 now
where the time goes in v1:
time: 111 us
  starting transfers between devices  41.1 us (37%)
  Pallas kernels  33.7 us (30%)
  waiting for transfers between devices  26.5 us (24%)
  matrix products  4.35 us (4%)
  local copies, waits for them, and re-layouts  3.96 us (4%)
    pallas_call x6, Pallas kernels, run(): pl.pallas_call(kernel, out_shape=outs, in_specs=[place] * len(args), out_...  33.7 us
    all_to_all x2, starting transfers between devices, exchange(): return lax.all_to_all(row, ALL, 0, 0, tiled=True)  23.4 us
    all_to_all x2, waiting for transfers between devices, exchange(): return lax.all_to_all(row, ALL, 0, 0, tiled=True)  15.3 us
    ppermute x2, starting transfers between devices, neighbours(): before = lax.ppermute(down, 'fx', [(i, i + 1) for i in range(7)])  8.42 us
    ppermute x2, waiting for transfers between devices, neighbours(): before = lax.ppermute(down, 'fx', [(i, i + 1) for i in range(7)])  7.13 us
    ppermute x2, waiting for transfers between devices, neighbours(): after = lax.ppermute(up, 'fx', [(i + 1, i) for i in range(7)])  4.05 us
    ppermute x1, starting transfers between devices, sides(): right = lax.ppermute(pack, axes, [(i + 1, i) for i in range(31)])  3.6 us
    ppermute x1, starting transfers between devices, sides(): left = lax.ppermute(pack, axes, [(i, i + 1) for i in range(31)])  3.1 us
  transfers between devices with their start and end apart: 8, of which 4 were waited for; matrix products, arithmetic and copies ran while one was open for 5% of the time, Pallas kernels for 7%

profile of v1, /device:TPU:1, one launch (start us, length us, event | category | flops | bytes accessed | tf_op | source)
XLA Modules:
  0.0 110.6 jit_solution(12354035494111539463)
XLA Ops:
  0.6 0.0 copy-start
  0.6 2.9 %shard_map.139 = (f32[128,8,128]{2,1,0:T(8,128)}, f32[128,8,128]{2,1,0:T(8,128)}) custom-call(f32[3,32,16,128]{3,2,1,0:T(8,128)} %refs_0_.1, f32[3,32,16,128]{3,2,1,0:T(8,128)} %refs_1_.1, f32[32,16,128]{2,1,0:T(8,128)} %refs_2_.3, f32[32,16,128]{2,1,0:T(8,128)} %refs_3_.3), custom_call_target="tpu_custom_call" | custom-call | flops 1000000 | bytes 1000000 | tf_op jit(solution)/shard_map/pallas_call | solution.py:479
  3.5 4.4 %collective-permute-start.1 = (f32[128,8,128]{2,1,0:T(8,128)}, f32[128,8,128]{2,1,0:T(8,128)S(1)}, u32[]{:S(2)}, u32[]{:S(2)}) collective-permute-start(f32[128,8,128]{2,1,0:T(8,128)} %get-tuple-element.19), channel_id=1, source_target_pairs={{0,32},{32,64},{64,96},{96,128},{128,160},{160,192},{192,224},{1,3... | collective-permute-start | bytes 1572872 | tf_op jit(solution)/shard_map/ppermute | solution.py:494
  7.9 1.3 %collective-permute-start = (f32[128,8,128]{2,1,0:T(8,128)}, f32[128,8,128]{2,1,0:T(8,128)S(1)}, u32[]{:S(2)}, u32[]{:S(2)}) collective-permute-start(f32[128,8,128]{2,1,0:T(8,128)} %get-tuple-element.18.after_hbm), channel_id=1, source_target_pairs={{32,0},{64,32},{96,64},{128,96},{160,128},{192,160},{224,192},{33,... | collective-permute-start | bytes 1572872 | tf_op jit(solution)/shard_map/ppermute | solution.py:493
  9.2 2.4 %shard_map.140 = (f32[256,128]{1,0:T(8,128)}, f32[1,128]{1,0:T(1,128)}) custom-call(f32[2,2,8]{2,1,0:T(2,128)} %bitcast.32, f32[3,32,16,128]{3,2,1,0:T(8,128)} %refs_0_.1, s32[1,32]{1,0:T(1,128)} %refs_11_.3, f32[8,256]{1,0:T(8,128)} %state_hbm.1, f32[8,2,256]{2,1,0:T(2,128)} %refs_15_.3, f32[128,8,128]{2,1,0:T(8,128)} %get-tuple-element.18.after_hbm), custom_call_target="tpu_custom_call" | custom-call | flops 1000000 | bytes 1000000 | tf_op jit(solution)/shard_map/pallas_call | solution.py:479
  11.7 0.0 copy-start.9
  11.7 7.1 %collective-permute-done.1.before_hbm = f32[128,8,128]{2,1,0:T(8,128)S(1)} collective-permute-done((f32[128,8,128]{2,1,0:T(8,128)}, f32[128,8,128]{2,1,0:T(8,128)S(1)}, u32[]{:S(2)}, u32[]{:S(2)}) %collective-permute-start.1) | collective-permute-done | bytes 524320 | tf_op jit(solution)/shard_map/ppermute | solution.py:494
  18.8 0.0 copy-start.4
  18.8 4.0 %collective-permute-done.after_hbm = f32[128,8,128]{2,1,0:T(8,128)S(1)} collective-permute-done((f32[128,8,128]{2,1,0:T(8,128)}, f32[128,8,128]{2,1,0:T(8,128)S(1)}, u32[]{:S(2)}, u32[]{:S(2)}) %collective-permute-start) | collective-permute-done | bytes 524320 | tf_op jit(solution)/shard_map/ppermute | solution.py:493
  22.9 0.0 copy-start.5
  22.9 0.0 copy-done.4
  22.9 0.8 copy-done.5
  23.6 3.9 %shard_map.141 = (f32[8,32,8,128]{3,2,1,0:T(8,128)}, f32[8,24,512]{2,1,0:T(8,128)}) custom-call(f32[3,32,16,128]{3,2,1,0:T(8,128)} %refs_0_.1, f32[3,32,16,128]{3,2,1,0:T(8,128)} %refs_1_.1, f32[32,16,128]{2,1,0:T(8,128)} %refs_2_.3, f32[32,16,128]{2,1,0:T(8,128)} %refs_3_.3, f32[128,8,128]{2,1,0:T(8,128)} %copy-done.5, f32[128,8,128]{2,1,0:T(8,128)} %copy-done.4, ...), custom_call_target="tpu_custom_call" | custom-call | flops 1000000 | bytes 1000000 | tf_op jit(solution)/shard_map/pallas_call | solution.py:479
  27.5 3.6 %collective-permute-start.3 = (f32[8,24,512]{2,1,0:T(8,128)}, f32[8,24,512]{2,1,0:T(8,128)S(1)}, u32[]{:S(2)}, u32[]{:S(2)}) collective-permute-start(f32[8,24,512]{2,1,0:T(8,128)} %get-tuple-element.22.refs_5_), channel_id=1, source_target_pairs={{1,0},{2,1},{3,2},{4,3},{5,4},{6,5},{7,6},{8,7},{9,8},{10,9},{11,1... | collective-permute-start | bytes 1179656 | tf_op jit(solution)/shard_map/ppermute | solution.py:501
  31.1 3.1 %collective-permute-start.2 = (f32[8,24,512]{2,1,0:T(8,128)}, f32[8,24,512]{2,1,0:T(8,128)S(1)}, u32[]{:S(2)}, u32[]{:S(2)}) collective-permute-start(f32[8,24,512]{2,1,0:T(8,128)} %get-tuple-element.22.refs_5_), channel_id=1, source_target_pairs={{0,1},{1,2},{2,3},{3,4},{4,5},{5,6},{6,7},{7,8},{8,9},{9,10},{10,1... | collective-permute-start | bytes 1179656 | tf_op jit(solution)/shard_map/ppermute | solution.py:500
  34.2 14.6 %all-to-all-start = ((f32[256,1,128]{2,1,0:T(1,128)}), f32[256,1,128]{2,1,0:T(1,128)S(1)}, u32[]{:S(2)}, u32[]{:S(2)}) async-start(f32[256,1,128]{2,1,0:T(1,128)} %bitcast.2), calls=%async_computation | async-start | bytes 262144 | tf_op jit(solution)/shard_map/all_to_all | solution.py:506
  48.8 0.0 copy-done
  48.8 0.0 copy-done.9
  48.8 1.8 %fusion.2 = f32[8,1,256]{2,1,0:T(1,128)S(1)} fusion(f32[8,256,256]{2,1,0:T(8,128)S(1)} %copy-done, f32[8,256,1]{1,0,2:T(8,128)S(1)} %bitcast.27), kind=kOutput, calls=%fused_computation.4 | convolution fusion | flops 6291456 | bytes 2113536 | tf_op jit(solution)/shard_map/mpr,mr->mp/dot_general | solution.py:540
  50.7 0.6 copy.28
  51.3 5.0 %shard_map.142 = (bf16[880,256]{1,0:T(8,128)(2,1)}, f32[1744,128]{1,0:T(8,128)}) custom-call(s32[1,256]{1,0:T(1,128)} %bitcast.33, s32[32,128]{1,0:T(8,128)} %bitcast.30), custom_call_target="tpu_custom_call" | custom-call | flops 1000000 | bytes 1000000 | tf_op jit(solution)/shard_map/pallas_call | solution.py:479
  56.3 5.5 %all-to-all-done = f32[256,1,128]{2,1,0:T(1,128)S(1)} async-done(((f32[256,1,128]{2,1,0:T(1,128)}), f32[256,1,128]{2,1,0:T(1,128)S(1)}, u32[]{:S(2)}, u32[]{:S(2)}) %all-to-all-start) | async-done | bytes 131104 | tf_op jit(solution)/shard_map/all_to_all | solution.py:506
  61.8 0.0 copy-start.6
  61.8 0.0 collective-permute-done.3.refs_7_
  61.8 0.0 copy-start.1
  61.8 0.0 collective-permute-done.2.refs_6_
  61.8 0.0 copy-start.2
  61.8 0.6 copy-done.6
  62.4 0.2 copy-done.1
  62.6 0.1 copy-done.2
  62.7 9.9 %shard_map.143 = (f32[3,32,16,128]{3,2,1,0:T(8,128)}, f32[3,32,16,128]{3,2,1,0:T(8,128)}, f32[8,256]{1,0:T(8,128)}, f32[256,128]{1,0:T(8,128)}, f32[120,8,128]{2...) custom-call(f32[3,32,16,128]{3,2,1,0:T(8,128)} %refs_0_.1, f32[3,32,16,128]{3,2,1,0:T(8,128)} %refs_1_.1, ...), custom_call_target="tpu_custom_call" | custom-call | flops 1000000 | bytes 1000000 | tf_op jit(solution)/shard_map/pallas_call | solution.py:479
  72.7 1.3 %collective-permute-start.4 = (f32[120,8,128]{2,1,0:T(8,128)}, f32[120,8,128]{2,1,0:T(8,128)S(1)}, u32[]{:S(2)}, u32[]{:S(2)}) collective-permute-start(f32[120,8,128]{2,1,0:T(8,128)} %get-tuple-element.31), channel_id=1, source_target_pairs={{32,0},{64,32},{96,64},{128,96},{160,128},{192,160},{224,192},{33,... | collective-permute-start | bytes 1474568 | tf_op jit(solution)/shard_map/ppermute | solution.py:493
  74.0 4.0 %collective-permute-start.5 = (f32[120,8,128]{2,1,0:T(8,128)}, f32[120,8,128]{2,1,0:T(8,128)S(1)}, u32[]{:S(2)}, u32[]{:S(2)}) collective-permute-start(f32[120,8,128]{2,1,0:T(8,128)} %get-tuple-element.32), channel_id=1, source_target_pairs={{0,32},{32,64},{64,96},{96,128},{128,160},{160,192},{192,224},{1,3... | collective-permute-start | bytes 1474568 | tf_op jit(solution)/shard_map/ppermute | solution.py:494
  78.0 8.8 %all-to-all-start.1 = ((f32[256,1,128]{2,1,0:T(1,128)}), f32[256,1,128]{2,1,0:T(1,128)S(1)}, u32[]{:S(2)}, u32[]{:S(2)}) async-start(f32[256,1,128]{2,1,0:T(1,128)} %bitcast.24), calls=%async_computation.1 | async-start | bytes 262144 | tf_op jit(solution)/shard_map/all_to_all | solution.py:506
  86.8 2.5 %fusion = f32[8,1,256]{2,1,0:T(1,128)S(1)} fusion(f32[8,256,256]{2,1,0:T(8,128)S(1)} %copy-done, f32[8,256,1]{1,0,2:T(8,128)} %bitcast.31), kind=kOutput, calls=%fused_computation.1 | convolution fusion | flops 6291456 | bytes 2113536 | tf_op jit(solution)/shard_map/mpr,mr->mp/dot_general | solution.py:560
  89.3 0.6 copy.27
  89.9 9.9 %all-to-all-done.1 = f32[256,1,128]{2,1,0:T(1,128)S(1)} async-done(((f32[256,1,128]{2,1,0:T(1,128)}), f32[256,1,128]{2,1,0:T(1,128)S(1)}, u32[]{:S(2)}, u32[]{:S(2)}) %all-to-all-start.1) | async-done | bytes 131104 | tf_op jit(solution)/shard_map/all_to_all | solution.py:506
  99.8 0.0 copy-start.3
  99.8 0.0 collective-permute-done.4.refs_17_
  99.8 0.0 copy-start.7
  99.8 0.0 collective-permute-done.5.refs_18_
  99.8 0.0 copy-start.8
  99.8 0.6 copy-done.3
  100.4 0.2 copy-done.7
  100.6 0.2 copy-done.8
  100.8 9.6 %shard_map.144 = (f32[3,32,16,128]{3,2,1,0:T(8,128)}, f32[3,32,16,128]{3,2,1,0:T(8,128)}, f32[8,256]{1,0:T(8,128)}) custom-call(f32[3,32,16,128]{3,2,1,0:T(8,128)} %get-tuple-element.26.refs_0_, f32[3,32,16,128]{3,2,1,0:T(8,128)} %get-tuple-element.27.refs_1_, f32[32,16,128]{2,1,0:T(8,128)} %refs_2_.3, f32[32,16,128]{2,1,0:T(8,128)} %refs_3_.3, ...), custom_call_target="tpu_custom_call" | custom-call | flops 1000000 | bytes 1000000 | tf_op jit(solution)/shard_map/pallas_call | solution.py:479
Async XLA Ops:
  0.6 48.2 %copy-start = (f32[8,256,256]{2,1,0:T(8,128)S(1)}, f32[8,256,256]{2,1,0:T(8,128)}, u32[]{:S(2)}) copy-start(f32[8,256,256]{2,1,0:T(8,128)} %param.20) | copy-start | bytes 6291460
  3.5 15.3 %collective-permute-start.1 = (f32[128,8,128]{2,1,0:T(8,128)}, f32[128,8,128]{2,1,0:T(8,128)S(1)}, u32[]{:S(2)}, u32[]{:S(2)}) collective-permute-start(f32[128,8,128]{2,1,0:T(8,128)} %get-tuple-element.19), channel_id=1, source_target_pairs={{0,32},{32,64},{64,96},{96,128},{128,160},{160,192},{192,224},{1,3... | collective-permute-start | bytes 1572872 | tf_op jit(solution)/shard_map/ppermute | solution.py:494
  7.9 14.9 %collective-permute-start = (f32[128,8,128]{2,1,0:T(8,128)}, f32[128,8,128]{2,1,0:T(8,128)S(1)}, u32[]{:S(2)}, u32[]{:S(2)}) collective-permute-start(f32[128,8,128]{2,1,0:T(8,128)} %get-tuple-element.18.after_hbm), channel_id=1, source_target_pairs={{32,0},{64,32},{96,64},{128,96},{160,128},{192,160},{224,192},{33,... | collective-permute-start | bytes 1572872 | tf_op jit(solution)/shard_map/ppermute | solution.py:493
  11.7 37.2 %copy-start.9 = (f32[8,256]{1,0:T(8,128)S(1)}, f32[8,256]{1,0:T(8,128)}, u32[]{:S(2)}) copy-start(f32[8,256]{1,0:T(8,128)} %state_hbm.1) | copy-start | bytes 24580
  18.8 4.1 %copy-start.4 = (f32[128,8,128]{2,1,0:T(8,128)}, f32[128,8,128]{2,1,0:T(8,128)S(1)}, u32[]{:S(2)}) copy-start(f32[128,8,128]{2,1,0:T(8,128)S(1)} %collective-permute-done.1.before_hbm) | copy-start | bytes 1572868
  22.9 0.8 copy-start.5
  27.5 34.3 %collective-permute-start.3 = (f32[8,24,512]{2,1,0:T(8,128)}, f32[8,24,512]{2,1,0:T(8,128)S(1)}, u32[]{:S(2)}, u32[]{:S(2)}) collective-permute-start(f32[8,24,512]{2,1,0:T(8,128)} %get-tuple-element.22.refs_5_), channel_id=1, source_target_pairs={{1,0},{2,1},{3,2},{4,3},{5,4},{6,5},{7,6},{8,7},{9,8},{10,9},{11,1... | collective-permute-start | bytes 1179656 | tf_op jit(solution)/shard_map/ppermute | solution.py:501
  31.1 30.7 %collective-permute-start.2 = (f32[8,24,512]{2,1,0:T(8,128)}, f32[8,24,512]{2,1,0:T(8,128)S(1)}, u32[]{:S(2)}, u32[]{:S(2)}) collective-permute-start(f32[8,24,512]{2,1,0:T(8,128)} %get-tuple-element.22.refs_5_), channel_id=1, source_target_pairs={{0,1},{1,2},{2,3},{3,4},{4,5},{5,6},{6,7},{7,8},{8,9},{9,10},{10,1... | collective-permute-start | bytes 1179656 | tf_op jit(solution)/shard_map/ppermute | solution.py:500
  34.2 27.5 %all-to-all-start = ((f32[256,1,128]{2,1,0:T(1,128)}), f32[256,1,128]{2,1,0:T(1,128)S(1)}, u32[]{:S(2)}, u32[]{:S(2)}) async-start(f32[256,1,128]{2,1,0:T(1,128)} %bitcast.2), calls=%async_computation | async-start | bytes 262144 | tf_op jit(solution)/shard_map/all_to_all | solution.py:506
  61.8 0.6 copy-start.6
  61.8 0.8 copy-start.1
  61.8 0.9 copy-start.2
  72.7 27.1 %collective-permute-start.4 = (f32[120,8,128]{2,1,0:T(8,128)}, f32[120,8,128]{2,1,0:T(8,128)S(1)}, u32[]{:S(2)}, u32[]{:S(2)}) collective-permute-start(f32[120,8,128]{2,1,0:T(8,128)} %get-tuple-element.31), channel_id=1, source_target_pairs={{32,0},{64,32},{96,64},{128,96},{160,128},{192,160},{224,192},{33,... | collective-permute-start | bytes 1474568 | tf_op jit(solution)/shard_map/ppermute | solution.py:493
  74.0 25.8 %collective-permute-start.5 = (f32[120,8,128]{2,1,0:T(8,128)}, f32[120,8,128]{2,1,0:T(8,128)S(1)}, u32[]{:S(2)}, u32[]{:S(2)}) collective-permute-start(f32[120,8,128]{2,1,0:T(8,128)} %get-tuple-element.32), channel_id=1, source_target_pairs={{0,32},{32,64},{64,96},{96,128},{128,160},{160,192},{192,224},{1,3... | collective-permute-start | bytes 1474568 | tf_op jit(solution)/shard_map/ppermute | solution.py:494
  78.0 21.8 %all-to-all-start.1 = ((f32[256,1,128]{2,1,0:T(1,128)}), f32[256,1,128]{2,1,0:T(1,128)S(1)}, u32[]{:S(2)}, u32[]{:S(2)}) async-start(f32[256,1,128]{2,1,0:T(1,128)} %bitcast.24), calls=%async_computation.1 | async-start | bytes 262144 | tf_op jit(solution)/shard_map/all_to_all | solution.py:506
  99.8 0.7 copy-start.3
  99.8 0.8 copy-start.7
  99.8 1.0 copy-start.8
